TPU v7x, 32 devices: a whole 2x2x4 slice. The times are simulated.
32 devices in a mesh: ia: 2 (over x), ja: 4 (over y, core), ka: 4 (over z).
Axes of the slice: x: 2, y: 2, z: 4, core: 2. Of those that a mesh axis runs over, the one named last changes fastest.
Arguments:
- pre_act: bfloat16 [1024, 24576], P('ia', ('ja', 'ka')), may hold values from -6 to 6
- down_weight: bfloat16 [6144, 24576], P(('ka', 'ia'), 'ja'), may hold values from -0.0546875 to 0.0546875
- grad_out: bfloat16 [1024, 6144], P('ia', ('ka', 'ja')), may hold values from -6 to 6
Outputs:
- output: bfloat16 [1024, 6144], P('ia', ('ka', 'ja'))
- grad_pre: bfloat16 [1024, 24576], P('ia', ('ja', 'ka'))
- grad_weight: bfloat16 [6144, 24576], P(('ka', 'ia'), 'ja')
All inputs are finite; a program needn't handle non-finite values.
Results may differ from a plain program's by a relative error of at most 0.02.
Values may be sent and summed in bfloat16 or wider, within the bound.
A program may use at most 128 MiB of HBM per device.

v0:
```python
import jax
import jax.numpy as jnp
from jax import lax
from jax.sharding import PartitionSpec as P

coeff = 0.7978845608028654


def gelu_value(v):
    return 0.5 * v * (1.0 + jnp.tanh(coeff * (v + 0.044715 * v * v * v)))


def gelu_slope(v):
    tval = jnp.tanh(coeff * (v + 0.044715 * v * v * v))
    return 0.5 * (1.0 + tval) + 0.5 * v * (1.0 - tval * tval) * coeff * (
        1.0 + 3.0 * 0.044715 * v * v
    )


def shards(pre_act, down_weight, grad_out):
    pre32 = pre_act.astype(jnp.float32)
    pre_block = lax.all_gather(pre_act, "ka", axis=1, tiled=True)
    hidden = gelu_value(pre_block.astype(jnp.float32)).astype(jnp.bfloat16)
    grad_block = lax.all_gather(grad_out, "ja", axis=1, tiled=True)
    weight_block = lax.all_gather(down_weight, "ia", axis=0, tiled=True)
    out_terms = lax.dot_general(
        hidden, weight_block, (((1,), (1,)), ((), ())), preferred_element_type=jnp.float32
    )
    hidden_terms = jnp.dot(grad_block, weight_block, preferred_element_type=jnp.float32)
    output = lax.psum_scatter(out_terms.astype(jnp.bfloat16), "ja", scatter_dimension=1, tiled=True)
    grad_hidden = lax.psum_scatter(
        hidden_terms.astype(jnp.bfloat16), "ka", scatter_dimension=1, tiled=True
    ).astype(jnp.float32)
    grad_pre = (grad_hidden * gelu_slope(pre32)).astype(jnp.bfloat16)
    weight_terms = lax.dot_general(
        grad_block, hidden, (((0,), (0,)), ((), ())), preferred_element_type=jnp.float32
    )
    grad_weight = lax.psum_scatter(
        weight_terms.astype(jnp.bfloat16), "ia", scatter_dimension=0, tiled=True
    )
    return (output, grad_pre, grad_weight)


def solution(mesh):
    placed = (P("ia", ("ja", "ka")), P(("ka", "ia"), "ja"), P("ia", ("ka", "ja")))
    return jax.shard_map(
        shards,
        mesh=mesh,
        in_specs=placed,
        out_specs=(P("ia", ("ka", "ja")), P("ia", ("ja", "ka")), P(("ka", "ia"), "ja")),
        check_vma=False,
    )
```

profile of v0, /device:TPU:27, one launch (start us, length us, event | category | flops | bytes accessed | tf_op | source)
XLA Modules:
  0.0 749.1 jit_solution(4261851703837757619)
XLA Ops:
  7.2 0.0 all-gather.4.cloned.1.call-start
  7.2 0.7 all-gather.4.cloned.1.call-update
  7.9 0.0 all-gather.6.cloned.1.call-start
  7.9 0.7 all-gather.6.cloned.1.call-update
  8.6 0.0 all-gather.8.cloned.1.call-start
  8.7 0.7 all-gather.8.cloned.1.call-update
  9.4 0.0 reduce-scatter.10.cloned.1.call-start
  9.4 113.9 %all-gather.4.cloned.1.call-done = bf16[512,6144]{1,0:T(8,128)(2,1)} async-done(((bf16[512,1536]{1,0:T(8,128)(2,1)}), bf16[512,6144]{1,0:T(8,128)(2,1)}) %all-gather.4.cloned.1.call-update) | async-done | bytes 6291472 | tf_op jit(solution)/shard_map/all_gather | solution.py:22
  123.3 225.8 %all-gather.6.cloned.1.call-done = bf16[1536,6144]{1,0:T(8,128)(2,1)} async-done(((bf16[768,6144]{1,0:T(8,128)(2,1)}), bf16[1536,6144]{1,0:T(8,128)(2,1)}) %all-gather.6.cloned.1.call-update) | async-done | bytes 18874384 | tf_op jit(solution)/shard_map/all_gather | solution.py:25
  349.1 21.2 %convolution_convert_fusion.2 = bf16[512,1536]{1,0:T(8,128)(2,1)S(1)} fusion(bf16[1536,6144]{1,0:T(8,128)(2,1)} %all-gather.6.cloned.1.call-done, bf16[512,6144]{1,0:T(8,128)(2,1)} %all-gather.4.cloned.1.call-done), kind=kOutput, calls=%fused_computation.29 | convolution fusion | flops 9695920128 | bytes 26738688 | tf_op jit(solution)/shard_map/dot_general | solution.py:26
  370.4 1.6 copy.8
  371.9 0.0 reduce-scatter.10.cloned.1.call-update
  372.0 0.0 reduce-scatter.6.cloned.1.call-start
  372.0 0.0 all-gather.8.cloned.1.call-done
  372.0 15.9 %convolution_convert_fusion.1 = bf16[512,6144]{1,0:T(8,128)(2,1)} fusion(bf16[512,1536]{1,0:T(8,128)(2,1)} %all-gather.8.cloned.1.call-done, bf16[1536,6144]{1,0:T(8,128)(2,1)} %all-gather.6.cloned.1.call-done), kind=kOutput, calls=%fused_computation.12 | convolution fusion | flops 9666822144 | bytes 26738688 | tf_op jit(solution)/shard_map/dot_general | solution.py:29
  387.9 0.0 copy-start.1
  387.9 0.0 reduce-scatter.6.cloned.1.call-update
  387.9 0.2 reduce-scatter.8.cloned.1.call-start
  388.2 1.2 copy-done.1
  389.3 21.8 %fusion = bf16[1536,6144]{0,1:T(8,128)(2,1)} fusion(bf16[512,1536]{1,0:T(8,128)(2,1)S(1)} %copy-done.1, bf16[512,6144]{1,0:T(8,128)(2,1)} %all-gather.4.cloned.1.call-done), kind=kOutput, calls=%fused_computation.6 | convolution fusion | flops 9704570880 | bytes 26738688 | tf_op jit(solution)/shard_map/dot_general | solution.py:35
  411.1 0.0 copy-start
  411.1 0.0 reduce-scatter.8.cloned.1.call-update
  411.1 0.0 reduce-scatter.10.cloned.1.call-done
  411.2 2.1 copy.9
  413.3 102.3 %reduce-scatter.6.cloned.1.call-done = bf16[512,1536]{1,0:T(8,128)(2,1)} async-done(((bf16[512,6144]{1,0:T(8,128)(2,1)}), bf16[512,1536]{1,0:T(8,128)(2,1)}) %reduce-scatter.6.cloned.1.call-update) | async-done | bytes 1572880 | tf_op jit(solution)/shard_map/reduce_scatter | solution.py:31
  515.6 0.0 copy-done
  515.6 4.2 fusion.13
  519.9 209.8 %reduce-scatter.8.cloned.1.call-done = bf16[768,6144]{0,1:T(8,128)(2,1)} async-done(((bf16[1536,6144]{0,1:T(8,128)(2,1)}), bf16[768,6144]{0,1:T(8,128)(2,1)}) %reduce-scatter.8.cloned.1.call-update) | async-done | bytes 9437200 | tf_op jit(solution)/shard_map/reduce_scatter | solution.py:38
  729.7 12.6 %copy.7 = bf16[768,6144]{1,0:T(8,128)(2,1)} copy(bf16[768,6144]{0,1:T(8,128)(2,1)} %reduce-scatter.8.cloned.1.call-done) | data formatting | bytes 18874368
Async XLA Ops:
  7.2 116.1 %all-gather.4.cloned.1.call-start = ((), (), s32[]{:S(2)}) async-start(), calls=%async_computation.3 | async-start | bytes 7864320 | tf_op jit(solution)/shard_map/all_gather | solution.py:22
  7.9 341.2 %all-gather.6.cloned.1.call-start = ((), (), s32[]{:S(2)}) async-start(), calls=%async_computation.4 | async-start | bytes 28311552 | tf_op jit(solution)/shard_map/all_gather | solution.py:25
  8.6 363.4 %all-gather.8.cloned.1.call-start = ((), (), s32[]{:S(2)}) async-start(), calls=%async_computation.5 | async-start | bytes 1966080 | tf_op jit(solution)/shard_map/all_gather | solution.py:24
  9.4 401.8 %reduce-scatter.10.cloned.1.call-start = ((), (), s32[]{:S(2)}) async-start(), calls=%async_computation.8 | async-start | bytes 1966080
  372.0 143.7 %reduce-scatter.6.cloned.1.call-start = ((), (), s32[]{:S(2)}) async-start(), calls=%async_computation.6 | async-start | bytes 7864320 | tf_op jit(solution)/shard_map/reduce_scatter | solution.py:31
  387.9 1.4 copy-start.1
  387.9 341.7 %reduce-scatter.8.cloned.1.call-start = ((), (), s32[]{:S(2)}) async-start(), calls=%async_computation.7 | async-start | bytes 28311552 | tf_op jit(solution)/shard_map/reduce_scatter | solution.py:38
  411.1 104.5 %copy-start = (bf16[512,1536]{1,0:T(8,128)(2,1)S(1)}, bf16[512,1536]{1,0:T(8,128)(2,1)}, u32[]{:S(2)}) copy-start(bf16[512,1536]{1,0:T(8,128)(2,1)} %param.3) | copy-start | bytes 4718596
Sparse Core Ops, SparseCore 0:
  9.6 113.6 all-gather.3
  124.9 224.2 all-gather.5
  350.7 20.9 all-gather.7
  374.7 27.7 reduce-scatter.9
  405.3 110.2 reduce-scatter.5
  517.9 211.7 reduce-scatter.7
where the time goes:
time: 752 us; the launch traced here: 749 us
  waiting for transfers between devices  654 us (87%)
  matrix products  58.9 us (8%)
  local copies, waits for them, and re-layouts  17.5 us (2%)
  between operations  14.1 us (2%)
    all_gather x1, waiting for transfers between devices, shards(): weight_block = lax.all_gather(down_weight, 'ia', axis=0, tiled=True)  226 us
    reduce_scatter x1, waiting for transfers between devices, shards(): lax.psum_scatter(weight_terms.astype(jnp.bfloat16), 'ia', scatter_dimensi...  210 us
    all_gather x1, waiting for transfers between devices, shards(): pre_block = lax.all_gather(pre_act, 'ka', axis=1, tiled=True)  114 us
    reduce_scatter x1, waiting for transfers between devices, shards(): lax.psum_scatter(hidden_terms.astype(jnp.bfloat16), 'ka', scatter_dimensi...  102 us
    dot_general x1, matrix products, shards(): lax.dot_general(grad_block, hidden, (((0,), (0,)), ((), ())), preferred_e...  21.8 us
    dot_general x1, matrix products, shards(): lax.dot_general(hidden, weight_block, (((1,), (1,)), ((), ())), preferred...  21.2 us
    unnamed x7, local copies, waits for them, and re-layouts  17.5 us
    dot_general x1, matrix products, shards(): jnp.dot(grad_block, weight_block, preferred_element_type=jnp.float32)  15.9 us
  transfers between devices with their start and end apart: 6, of which 4 were waited for; matrix products, arithmetic and copies ran while one was open for 9% of the time, Pallas kernels for 0%

commit v1 on v0

--- a/solution.py
+++ b/solution.py
@@ -41,10 +41,45 @@
     return (output, grad_pre, grad_weight)
 
 
+def stationary(pre_act, down_weight, grad_out):
+    pre32 = pre_act.astype(jnp.float32)
+    grad_block = lax.all_gather(grad_out, "ja", axis=1, tiled=True)
+    grad_block = lax.all_to_all(grad_block, "ia", split_axis=1, concat_axis=0, tiled=True)
+    pre_block = lax.all_gather(pre_act, "ka", axis=1, tiled=True)
+    pre_block = lax.all_gather(pre_block, "ia", axis=0, tiled=True)
+    hidden_terms = jnp.dot(grad_block, down_weight, preferred_element_type=jnp.float32)
+    grad_hidden = lax.psum_scatter(
+        hidden_terms.astype(jnp.bfloat16), "ia", scatter_dimension=0, tiled=True
+    )
+    grad_hidden = lax.psum_scatter(grad_hidden, "ka", scatter_dimension=1, tiled=True)
+    hidden = gelu_value(pre_block.astype(jnp.float32)).astype(jnp.bfloat16)
+    out_terms = lax.dot_general(
+        hidden, down_weight, (((1,), (1,)), ((), ())), preferred_element_type=jnp.float32
+    )
+    out_terms = lax.all_to_all(
+        out_terms.astype(jnp.bfloat16), "ia", split_axis=0, concat_axis=1, tiled=True
+    )
+    output = lax.psum_scatter(out_terms, "ja", scatter_dimension=1, tiled=True)
+    grad_weight = lax.dot_general(
+        grad_block, hidden, (((0,), (0,)), ((), ())), preferred_element_type=jnp.float32
+    ).astype(jnp.bfloat16)
+    grad_pre = (grad_hidden.astype(jnp.float32) * gelu_slope(pre32)).astype(jnp.bfloat16)
+    return (output, grad_pre, grad_weight)
+
+
+def pick(n_ia):
+    def chosen(pre_act, down_weight, grad_out):
+        if n_ia * down_weight.shape[0] > n_ia * pre_act.shape[0]:
+            return stationary(pre_act, down_weight, grad_out)
+        return shards(pre_act, down_weight, grad_out)
+
+    return chosen
+
+
 def solution(mesh):
     placed = (P("ia", ("ja", "ka")), P(("ka", "ia"), "ja"), P("ia", ("ka", "ja")))
     return jax.shard_map(
-        shards,
+        pick(mesh.shape["ia"]),
         mesh=mesh,
         in_specs=placed,
         out_specs=(P("ia", ("ka", "ja")), P("ia", ("ja", "ka")), P(("ka", "ia"), "ja")),

time: 752 us -> 625 us (0.83)
  waiting for transfers between devices: 654 us -> 462 us
  blocking collectives: 0 us -> 64.7 us
    reduce_scatter x2, waiting for transfers between devices: 312 us -> 210 us  [the longest x1 109 us: stationary(): lax.psum_scatter(grad_hidden, 'ka', scatter_dimension=1, tiled=True)]
    all_gather x3, waiting for transfers between devices: 340 us -> 251 us  [the longest x1 115 us: stationary(): pre_block = lax.all_gather(pre_block, 'ia', axis=0, tiled=True)]
    all_to_all x0 -> x2, blocking collectives: none -> 64.7 us  [the longest x1 39 us: stationary(): lax.all_to_all(out_terms.astype(jnp.bfloat16), 'ia', split_axis=0, concat...]
    unnamed x7 -> x6, local copies, waits for them, and re-layouts: 17.5 us -> 18.2 us
  transfers between devices with their start and end apart: 6 -> 6, of which waited for: 4 -> 5; matrix products, arithmetic and copies ran while one was open for 9% -> 12% of each run, Pallas kernels for 0% -> 0%
where the time goes in v1:
time: 625 us; the launch traced here: 622 us
  waiting for transfers between devices  462 us (74%)
  blocking collectives  64.7 us (10%)
  matrix products  58 us (9%)
  local copies, waits for them, and re-layouts  18.9 us (3%)
  between operations  14.1 us (2%)
    all_gather x1, waiting for transfers between devices, stationary(): pre_block = lax.all_gather(pre_block, 'ia', axis=0, tiled=True)  115 us
    all_gather x1, waiting for transfers between devices, stationary(): pre_block = lax.all_gather(pre_act, 'ka', axis=1, tiled=True)  113 us
    reduce_scatter x1, waiting for transfers between devices, stationary(): lax.psum_scatter(grad_hidden, 'ka', scatter_dimension=1, tiled=True)  109 us
    reduce_scatter x1, waiting for transfers between devices, stationary(): lax.psum_scatter(hidden_terms.astype(jnp.bfloat16), 'ia', scatter_dimensi...  101 us
    all_to_all x1, blocking collectives, stationary(): lax.all_to_all(out_terms.astype(jnp.bfloat16), 'ia', split_axis=0, concat...  39 us
    all_to_all x1, blocking collectives, stationary(): lax.all_to_all(grad_block, 'ia', split_axis=1, concat_axis=0, tiled=True)  25.7 us
    all_gather x1, waiting for transfers between devices, stationary(): grad_block = lax.all_gather(grad_out, 'ja', axis=1, tiled=True)  23 us
    dot_general x1, matrix products, stationary(): lax.dot_general(hidden, down_weight, (((1,), (1,)), ((), ())), preferred_...  21.2 us
  transfers between devices with their start and end apart: 6, of which 5 were waited for; matrix products, arithmetic and copies ran while one was open for 12% of the time, Pallas kernels for 0%

profile of v1, /device:TPU:27, one launch (start us, length us, event | category | flops | bytes accessed | tf_op | source)
XLA Modules:
  0.0 622.0 jit_solution(7127999485665234575)
XLA Ops:
  7.2 0.0 all-gather.4.cloned.1.call-start
  7.2 0.7 all-gather.4.cloned.1.call-update
  7.9 0.0 all-gather.8.cloned.1.call-start
  7.9 1.9 copy.15
  9.9 0.0 all-gather.8.cloned.1.call-update
  9.9 0.0 all-gather.6.cloned.1.call-start
  9.9 113.4 %all-gather.4.cloned.1.call-done = bf16[512,6144]{1,0:T(8,128)(2,1)} async-done(((bf16[512,1536]{1,0:T(8,128)(2,1)}), bf16[512,6144]{1,0:T(8,128)(2,1)}) %all-gather.4.cloned.1.call-update) | async-done | bytes 6291472 | tf_op jit(solution)/shard_map/all_gather | solution.py:48
  123.3 0.0 all-gather.6.cloned.1.call-update
  123.3 0.0 reduce-scatter.6.cloned.1.call-start
  123.4 23.0 %all-gather.8.cloned.1.call-done = bf16[512,1536]{0,1:T(8,128)(2,1)} async-done(((bf16[512,384]{0,1:T(8,128)(2,1)}), bf16[512,1536]{0,1:T(8,128)(2,1)}) %all-gather.8.cloned.1.call-update) | async-done | bytes 1572880 | tf_op jit(solution)/shard_map/all_gather | solution.py:46
  146.3 25.7 %all_to_all.38 = bf16[512,2,768]{0,2,1:T(8,128)(2,1)S(1)} all-to-all(bf16[512,2,768]{0,2,1:T(8,128)(2,1)} %bitcast.20), channel_id=1, replica_groups=mesh['ia'=2,'ja'=4,'ka'=4] {'ia'}, dimensions={1} | all-to-all | bytes 3145728 | tf_op jit(solution)/shard_map/all_to_all | solution.py:47
  172.0 0.7 copy.16
  172.7 16.0 %convolution_convert_fusion = bf16[1024,6144]{1,0:T(8,128)(2,1)} fusion(bf16[1024,768]{1,0:T(8,128)(2,1)S(1)} %bitcast.18, bf16[768,6144]{1,0:T(8,128)(2,1)} %param.4), kind=kOutput, calls=%fused_computation.10 | convolution fusion | flops 9669967872 | bytes 23592960 | tf_op jit(solution)/shard_map/dot_general | solution.py:50
  188.8 0.0 reduce-scatter.6.cloned.1.call-update
  188.8 0.0 reduce-scatter.10.cloned.1.call-start
  188.9 114.7 %all-gather.6.cloned.1.call-done = bf16[1024,6144]{1,0:T(8,128)(2,1)} async-done(((bf16[512,6144]{1,0:T(8,128)(2,1)}), bf16[1024,6144]{1,0:T(8,128)(2,1)}) %all-gather.6.cloned.1.call-update) | async-done | bytes 12582928 | tf_op jit(solution)/shard_map/all_gather | solution.py:49
  303.6 21.2 %convolution_convert_fusion.2 = bf16[1024,768]{1,0:T(8,128)(2,1)S(1)} fusion(bf16[768,6144]{1,0:T(8,128)(2,1)} %param.4, bf16[1024,6144]{1,0:T(8,128)(2,1)} %all-gather.6.cloned.1.call-done), kind=kOutput, calls=%fused_computation.29 | convolution fusion | flops 9727377408 | bytes 23592960 | tf_op jit(solution)/shard_map/dot_general | solution.py:56
  324.8 39.0 %all_to_all.39 = bf16[2,512,768]{2,1,0:T(8,128)(2,1)S(1)} all-to-all(bf16[2,512,768]{2,1,0:T(8,128)(2,1)S(1)} %bitcast.21), channel_id=1, replica_groups=mesh['ia'=2,'ja'=4,'ka'=4] {'ia'}, dimensions={0} | all-to-all | bytes 3145728 | tf_op jit(solution)/shard_map/all_to_all | solution.py:59
  363.8 1.6 copy.20
  365.3 0.0 reduce-scatter.10.cloned.1.call-update
  365.4 0.2 reduce-scatter.8.cloned.1.call-start
  365.6 100.6 %reduce-scatter.6.cloned.1.call-done = bf16[512,6144]{1,0:T(8,128)(2,1)} async-done(((bf16[1024,6144]{1,0:T(8,128)(2,1)}), bf16[512,6144]{1,0:T(8,128)(2,1)}) %reduce-scatter.6.cloned.1.call-update) | async-done | bytes 6291472 | tf_op jit(solution)/shard_map/reduce_scatter | solution.py:51
  466.2 0.0 reduce-scatter.8.cloned.1.call-update
  466.3 20.8 %fusion.5 = bf16[768,6144]{0,1:T(8,128)(2,1)} fusion(bf16[1024,768]{1,0:T(8,128)(2,1)S(1)} %bitcast.19, bf16[1024,6144]{1,0:T(8,128)(2,1)} %all-gather.6.cloned.1.call-done), kind=kOutput, calls=%fused_computation.12 | convolution fusion | flops 9731309568 | bytes 23592960 | tf_op jit(solution)/shard_map/dot_general | solution.py:63
  487.0 0.0 copy-start
  487.0 12.8 %copy.17 = bf16[768,6144]{1,0:T(8,128)(2,1)} copy(bf16[768,6144]{0,1:T(8,128)(2,1)} %fusion.5) | data formatting | bytes 18874368
  499.9 0.0 reduce-scatter.10.cloned.1.call-done
  499.9 1.9 copy.19
  501.8 109.1 %reduce-scatter.8.cloned.1.call-done = bf16[512,1536]{1,0:T(8,128)(2,1)} async-done(((bf16[512,6144]{1,0:T(8,128)(2,1)}), bf16[512,1536]{1,0:T(8,128)(2,1)}) %reduce-scatter.8.cloned.1.call-update) | async-done | bytes 1572880 | tf_op jit(solution)/shard_map/reduce_scatter | solution.py:54
  610.9 0.0 copy-done
  610.9 4.2 fusion.13
Async XLA Ops:
  7.2 116.1 %all-gather.4.cloned.1.call-start = ((), (), s32[]{:S(2)}) async-start(), calls=%async_computation.5 | async-start | bytes 7864320 | tf_op jit(solution)/shard_map/all_gather | solution.py:48
  7.9 138.4 %all-gather.8.cloned.1.call-start = ((), (), s32[]{:S(2)}) async-start(), calls=%async_computation.7 | async-start | bytes 1966080 | tf_op jit(solution)/shard_map/all_gather | solution.py:46
  9.9 293.7 %all-gather.6.cloned.1.call-start = ((), (), s32[]{:S(2)}) async-start(), calls=%async_computation.6 | async-start | bytes 18874368 | tf_op jit(solution)/shard_map/all_gather | solution.py:49
  123.3 342.9 %reduce-scatter.6.cloned.1.call-start = ((), (), s32[]{:S(2)}) async-start(), calls=%async_computation.8 | async-start | bytes 18874368 | tf_op jit(solution)/shard_map/reduce_scatter | solution.py:51
  188.8 311.0 %reduce-scatter.10.cloned.1.call-start = ((), (), s32[]{:S(2)}) async-start(), calls=%async_computation.10 | async-start | bytes 1966080
  365.4 245.6 %reduce-scatter.8.cloned.1.call-start = ((), (), s32[]{:S(2)}) async-start(), calls=%async_computation.9 | async-start | bytes 7864320 | tf_op jit(solution)/shard_map/reduce_scatter | solution.py:54
  487.0 123.9 %copy-start = (bf16[512,1536]{1,0:T(8,128)(2,1)S(1)}, bf16[512,1536]{1,0:T(8,128)(2,1)}, u32[]{:S(2)}) copy-start(bf16[512,1536]{1,0:T(8,128)(2,1)} %param.3) | copy-start | bytes 4718596
Sparse Core Ops, SparseCore 0:
  9.6 113.6 all-gather.3
  125.4 20.8 all-gather.7
  147.9 155.6 all-gather.5
  305.7 160.4 reduce-scatter.5
  469.2 29.0 reduce-scatter.9
  500.6 110.2 reduce-scatter.7

commit v2 on v0

--- a/solution.py
+++ b/solution.py
@@ -1,8 +1,13 @@
+import functools
+
 import jax
 import jax.numpy as jnp
 from jax import lax
+from jax.experimental import pallas as pl
+from jax.experimental.pallas import tpu as pltpu
 from jax.sharding import PartitionSpec as P
 
+MESH = pl.DeviceIdType.MESH
 coeff = 0.7978845608028654
 
 
@@ -41,10 +46,403 @@
     return (output, grad_pre, grad_weight)
 
 
+def kernel(
+    X, J, Z, ra, ct, rt,
+    pre, w_hbm, go, out, gp, gw,
+    w, pre_all, g, gt, part, r1, rza, rzb, rf, outp, outr, outx, gwt,
+    loc, gws, go_s, go_r, gb_s, gb_r, ag_s, ag_r, r1_s, r1_r, ra_s, ra_r, rb_s, rb_r,
+    rf_s, rf_r, op_s, op_r, ox_s, ox_r,
+):
+    x, j, z = lax.axis_index("ia"), lax.axis_index("ja"), lax.axis_index("ka")
+    px = 1 - x
+    _, _, tok, cols = pre_all.shape
+    fc = go.shape[1]
+    nb = J // X
+    home, b = lax.div(j, nb) == x, lax.rem(j, nb)
+    bcols = pl.ds(pl.multiple_of(b * fc, fc), fc)
+    to_px, to_right, to_left = {"ia": px}, {"ka": z + 1}, {"ka": z - 1}
+    has_left, has_right = z > 0, z < Z - 1
+    rows = (pl.ds(0, ra), pl.ds(ra, tok - ra))
+
+    def remote(src, dst, ss, rs, dev):
+        return pltpu.make_async_remote_copy(
+            src_ref=src, dst_ref=dst, send_sem=ss, recv_sem=rs, device_id=dev, device_id_type=MESH
+        )
+
+    def got(dst, rs):
+        remote(dst, dst, rs, rs, to_px).wait_recv()
+
+    barrier = pltpu.get_barrier_semaphore()
+
+    def greet(dev):
+        pl.semaphore_signal(barrier, inc=1, device_id=dev, device_id_type=MESH)
+
+    greet(to_px)
+    for q in range(1, J):
+        greet({"ja": lax.rem(j + q, J)})
+    pl.when(has_right)(lambda: greet(to_right))
+    pl.when(has_left)(lambda: greet(to_left))
+    w_in = pltpu.make_async_copy(w_hbm, w, loc.at[0])
+    w_in.start()
+    own_in = pltpu.make_async_copy(pre, pre_all.at[x, z], loc.at[1])
+    own_in.start()
+    pre_in = pltpu.make_async_copy(pre, gp, loc.at[2])
+    pre_in.start()
+    pl.semaphore_wait(barrier, J + has_right.astype(jnp.int32) + has_left.astype(jnp.int32))
+
+    ag_sent = []
+    devs = (to_right, to_left, to_px)
+
+    def ag_send(p, xs, s, t, cond, own=False):
+        def copy():
+            src = pre.at[rows[p]] if own else pre_all.at[xs, s, rows[p]]
+            return remote(
+                src, pre_all.at[xs, s, rows[p]], ag_s.at[p, xs, s, t], ag_r.at[p, xs, s], devs[t]
+            )
+
+        pl.when(cond)(lambda: copy().start())
+        ag_sent.append((cond, copy))
+
+    def ag_got(p, xs, s):
+        got(pre_all.at[xs, s, rows[p]], ag_r.at[p, xs, s])
+
+    always = z >= 0
+
+    def go_copy():
+        return remote(go, g.at[x, :, bcols], go_s.at[0], go_r.at[0], to_px)
+
+    go_in = pltpu.make_async_copy(go, g.at[x, :, bcols], loc.at[3])
+    pl.when(jnp.logical_not(home))(lambda: go_copy().start())
+    pl.when(home)(lambda: go_in.start())
+    ag_send(1, x, z, 2, always, True)
+    ag_send(0, x, z, 0, has_right, True)
+    ag_send(0, x, z, 1, has_left, True)
+    ag_send(0, x, z, 2, always, True)
+    ag_send(1, x, z, 0, has_right, True)
+    ag_send(1, x, z, 1, has_left, True)
+
+    def gb_copy(q):
+        return remote(
+            g.at[:, :, bcols], g.at[:, :, bcols], gb_s.at[q], gb_r.at[b], {"ja": lax.rem(j + q, J)}
+        )
+
+    @pl.when(home)
+    def _():
+        go_in.wait()
+        got(g.at[px, :, bcols], go_r.at[0])
+        for q in range(1, J):
+            gb_copy(q).start()
+
+    ag_got(1, px, z)
+    ag_send(1, px, z, 0, has_right)
+    ag_send(1, px, z, 1, has_left)
+
+    def ag_step(k):
+        for s, came, t, more in ((z - k, z >= k, 0, has_right), (z + k, z + k < Z, 1, has_left)):
+            pl.when(came)(lambda s=s: ag_got(0, x, s))
+            ag_send(0, x, s, 2, came)
+            ag_send(0, x, s, t, jnp.logical_and(came, more))
+            for xs in (x, px):
+                pl.when(came)(lambda s=s, xs=xs: ag_got(1, xs, s))
+                ag_send(1, xs, s, t, jnp.logical_and(came, more))
+
+    ag_step(1)
+
+    for bb in range(nb):
+        view = g.at[:, :, pl.ds(bb * fc, fc)]
+        pl.when(j != nb * x + bb)(lambda view=view, bb=bb: got(view, gb_r.at[bb]))
+    w_in.wait()
+
+    def r1_copy(d):
+        return remote(part.at[px, d, rows[0]], r1.at[d], r1_s.at[d], r1_r.at[d], to_px)
+
+    def terms(xs, i):
+        d = jnp.where(z >= Z // 2, i, Z - 1 - i)
+
+        def tile(c, carry):
+            wide = pl.ds(pl.multiple_of(d * cols + c * ct, ct), ct)
+            at = pl.ds(pl.multiple_of(c * ct, ct), ct)
+            value = jnp.dot(g[xs], w[:, wide], preferred_element_type=jnp.float32)
+            part[xs, d, :, at] = value.astype(jnp.bfloat16)
+            return carry
+
+        lax.fori_loop(0, cols // ct, tile, 0)
+        return d
+
+    def terms_px(i, carry):
+        r1_copy(terms(px, i)).start()
+        return carry
+
+    def terms_x(i, carry):
+        terms(x, i)
+        return carry
+
+    lax.fori_loop(0, Z, terms_px, 0)
+    lax.fori_loop(0, Z, terms_x, 0)
+
+    def add(dst, src, count):
+        def tile(r, carry):
+            at = pl.ds(pl.multiple_of(r * 16, 16), 16)
+            value = dst[at].astype(jnp.float32) + src[at].astype(jnp.float32)
+            dst[at] = value.astype(jnp.bfloat16)
+            return carry
+
+        lax.fori_loop(0, count // 16, tile, 0)
+
+    rs_sent = []
+
+    def take_a(d, slot):
+        got(rza.at[slot], ra_r.at[slot])
+        add(part.at[x, d, rows[0]], rza.at[slot], ra)
+
+    def take_b(xs, d, slot):
+        got(rzb.at[xs, slot], rb_r.at[xs, slot])
+        add(part.at[xs, d, rows[1]], rzb.at[xs, slot], tok - ra)
+
+    def take_1(d):
+        got(r1.at[d], r1_r.at[d])
+        add(part.at[x, d, rows[0]], r1.at[d], ra)
+
+    def rs_step(i):
+        for d, cond, more, slot, dev in (
+            (Z - 1 - i, Z - 1 - i > z, has_left, Z - 1 - i, to_right),
+            (i, i < z, has_right, jnp.where(z == i + 1, Z, i), to_left),
+        ):
+            for xs in (px, x):
+
+                def copy_b(xs=xs, d=d, slot=slot, dev=dev):
+                    return remote(
+                        part.at[xs, d, rows[1]], rzb.at[xs, slot],
+                        rb_s.at[xs, d], rb_r.at[xs, slot], dev,
+                    )
+
+                pl.when(jnp.logical_and(cond, more))(lambda xs=xs, d=d: take_b(xs, d, d))
+                pl.when(cond)(lambda copy_b=copy_b: copy_b().start())
+                rs_sent.append((cond, copy_b))
+
+            def copy_a(d=d, slot=slot, dev=dev):
+                return remote(
+                    part.at[x, d, rows[0]], rza.at[slot], ra_s.at[d], ra_r.at[slot], dev
+                )
+
+            pl.when(cond)(lambda d=d: take_1(d))
+            pl.when(jnp.logical_and(cond, more))(lambda d=d: take_a(d, d))
+            pl.when(cond)(lambda copy_a=copy_a: copy_a().start())
+            rs_sent.append((cond, copy_a))
+
+    mid = Z - 2
+    for k in range(2, Z):
+        ag_step(k)
+        if k - 2 < mid:
+            rs_step(k - 2)
+
+    for s in range(Z):
+        pl.when(z != s)(lambda s=s: ag_got(0, px, s))
+    ag_got(0, px, z)
+    own_in.wait()
+    for cond, copy in ag_sent:
+        pl.when(cond)(lambda copy=copy: copy().wait_send())
+
+    def act(n, carry):
+        xs, rest = lax.div(n, Z * (tok // 16)), lax.rem(n, Z * (tok // 16))
+        s, r = lax.div(rest, tok // 16), lax.rem(rest, tok // 16)
+        at = pl.ds(pl.multiple_of(r * 16, 16), 16)
+        pre_all[xs, s, at] = gelu_value(pre_all[xs, s, at].astype(jnp.float32)).astype(jnp.bfloat16)
+        return carry
+
+    lax.fori_loop(0, X * Z * (tok // 16), act, 0)
+
+    def out_tile(n, carry):
+        xs, r = lax.div(n, tok // rt), lax.rem(n, tok // rt)
+        at = pl.ds(pl.multiple_of(r * rt, rt), rt)
+        acc = None
+        for s in range(Z):
+            term = lax.dot_general(
+                pre_all[xs, s, at], w[:, s * cols : (s + 1) * cols], (((1,), (1,)), ((), ())),
+                preferred_element_type=jnp.float32,
+            )
+            acc = term if acc is None else acc + term
+        for bb in range(nb):
+            outp[bb, xs, at] = acc[:, bb * fc : (bb + 1) * fc].astype(jnp.bfloat16)
+        return carry
+
+    lax.fori_loop(0, X * (tok // rt), out_tile, 0)
+
+    def op_copy(bb):
+        jd = nb * x + bb
+        q = lax.rem(j - jd - 1 + J, J)
+        return remote(outp.at[bb], outr.at[q], op_s.at[bb], op_r.at[q], {"ja": jd})
+
+    for bb in range(nb):
+        pl.when(j != nb * x + bb)(lambda bb=bb: op_copy(bb).start())
+
+    for i in range(mid, Z - 1):
+        rs_step(i)
+
+    for xs in range(X):
+        gt[:, xs * tok : (xs + 1) * tok] = g[xs].T
+
+    n_tiles = Z * (cols // ct)
+
+    def gw_copy(n, slot):
+        wide = pl.ds(pl.multiple_of(n * ct, ct), ct)
+        return pltpu.make_async_copy(gwt.at[slot], gw.at[:, wide], gws.at[slot])
+
+    def gw_tile(n, carry):
+        slot = lax.rem(n, 2)
+        s, c = lax.div(n, cols // ct), lax.rem(n, cols // ct)
+        at = pl.ds(pl.multiple_of(c * ct, ct), ct)
+        pl.when(n >= 2)(lambda: gw_copy(n - 2, slot).wait())
+        acc = None
+        for xs in range(X):
+            term = jnp.dot(
+                gt[:, xs * tok : (xs + 1) * tok], pre_all[xs, s, :, at],
+                preferred_element_type=jnp.float32,
+            )
+            acc = term if acc is None else acc + term
+        gwt[slot] = acc.astype(jnp.bfloat16)
+        gw_copy(n, slot).start()
+        return carry
+
+    lax.fori_loop(0, n_tiles, gw_tile, 0)
+
+    def rf_copy():
+        return remote(part.at[px, z, rows[1]], rf, rf_s.at[0], rf_r.at[0], to_px)
+
+    for xs in (px, x):
+        pl.when(has_left)(lambda xs=xs: take_b(xs, z, z))
+        pl.when(has_right)(lambda xs=xs: take_b(xs, z, Z))
+        if xs is px:
+            rf_copy().start()
+    take_1(z)
+    pl.when(has_left)(lambda: take_a(z, z))
+    pl.when(has_right)(lambda: take_a(z, Z))
+
+    def ox_copy():
+        return remote(outp.at[b, px], outx, ox_s.at[0], ox_r.at[0], to_px)
+
+    @pl.when(home)
+    def _():
+        for q in range(J - 1):
+            got(outr.at[q], op_r.at[q])
+
+        def total(xs, r):
+            at = pl.ds(pl.multiple_of(r * 16, 16), 16)
+            value = outp[b, xs, at].astype(jnp.float32)
+            for q in range(J - 1):
+                value = value + outr[q, xs, at].astype(jnp.float32)
+            return at, value.astype(jnp.bfloat16)
+
+        def far(r, carry):
+            at, value = total(px, r)
+            outp[b, px, at] = value
+            return carry
+
+        def near(r, carry):
+            at, value = total(x, r)
+            out[at] = value
+            return carry
+
+        lax.fori_loop(0, tok // 16, far, 0)
+        ox_copy().start()
+        lax.fori_loop(0, tok // 16, near, 0)
+
+    pre_in.wait()
+
+    def slope(r, carry):
+        at = pl.ds(pl.multiple_of(r * 16, 16), 16)
+        value = part[x, z, at].astype(jnp.float32) * gelu_slope(gp[at].astype(jnp.float32))
+        gp[at] = value.astype(jnp.bfloat16)
+        return carry
+
+    lax.fori_loop(0, ra // 16, slope, 0)
+    got(rf, rf_r.at[0])
+    add(part.at[x, z, rows[1]], rf, tok - ra)
+    lax.fori_loop(ra // 16, tok // 16, slope, 0)
+
+    @pl.when(jnp.logical_not(home))
+    def _():
+        got(outx, ox_r.at[0])
+        out[...] = outx[...]
+        go_copy().wait_send()
+
+    @pl.when(home)
+    def _():
+        ox_copy().wait_send()
+        for q in range(1, J):
+            gb_copy(q).wait_send()
+
+    for bb in range(nb):
+        pl.when(j != nb * x + bb)(lambda bb=bb: op_copy(bb).wait_send())
+    rf_copy().wait_send()
+    for d in range(Z):
+        r1_copy(d).wait_send()
+    for cond, copy in rs_sent:
+        pl.when(cond)(lambda copy=copy: copy().wait_send())
+    for n in range(max(n_tiles - 2, 0), n_tiles):
+        gw_copy(n, n % 2).wait()
+
+
+def stationary(X, J, Z, pre_act, down_weight, grad_out):
+    tok, cols = pre_act.shape
+    feats, hid = down_weight.shape
+    fc = grad_out.shape[1]
+    ra = tok * 9 // 16 // 16 * 16
+    rb = tok - ra
+    ct = 512 if cols % 512 == 0 else 128
+    rt = 256 if tok % 256 == 0 else tok
+    nb = J // X
+    half = jnp.bfloat16
+    dma = pltpu.SemaphoreType.DMA
+    anywhere = pl.BlockSpec(memory_space=pl.ANY)
+    vmem = pl.BlockSpec(memory_space=pltpu.VMEM)
+    return pl.pallas_call(
+        functools.partial(kernel, X, J, Z, ra, ct, rt),
+        out_shape=(
+            jax.ShapeDtypeStruct((tok, fc), half),
+            jax.ShapeDtypeStruct((tok, cols), half),
+            jax.ShapeDtypeStruct((feats, hid), half),
+        ),
+        in_specs=[anywhere] * 3,
+        out_specs=(vmem, vmem, anywhere),
+        scratch_shapes=[
+            pltpu.VMEM((feats, hid), half),
+            pltpu.VMEM((X, Z, tok, cols), half),
+            pltpu.VMEM((X, tok, nb * fc), half),
+            pltpu.VMEM((nb * fc, X * tok), half),
+            pltpu.VMEM((X, Z, tok, cols), half),
+            pltpu.VMEM((Z, ra, cols), half),
+            pltpu.VMEM((Z + 1, ra, cols), half),
+            pltpu.VMEM((X, Z + 1, rb, cols), half),
+            pltpu.VMEM((rb, cols), half),
+            pltpu.VMEM((nb, X, tok, fc), half),
+            pltpu.VMEM((J - 1, X, tok, fc), half),
+            pltpu.VMEM((tok, fc), half),
+            pltpu.VMEM((2, feats, ct), half),
+            dma((4,)), dma((2,)), dma((1,)), dma((1,)), dma((J,)), dma((nb,)),
+            dma((2, X, Z, 3)), dma((2, X, Z)), dma((Z,)), dma((Z,)), dma((Z,)), dma((Z + 1,)),
+            dma((X, Z)), dma((X, Z + 1)), dma((1,)), dma((1,)), dma((nb,)), dma((J,)),
+            dma((1,)), dma((1,)),
+        ],
+        compiler_params=pltpu.CompilerParams(
+            collective_id=0, has_side_effects=True, vmem_limit_bytes=63 * 2**20
+        ),
+    )(pre_act, down_weight, grad_out)
+
+
+def pick(n_ia, n_ja, n_ka):
+    def chosen(pre_act, down_weight, grad_out):
+        if n_ia == 2 and down_weight.shape[0] > pre_act.shape[0]:
+            return stationary(n_ia, n_ja, n_ka, pre_act, down_weight, grad_out)
+        return shards(pre_act, down_weight, grad_out)
+
+    return chosen
+
+
 def solution(mesh):
     placed = (P("ia", ("ja", "ka")), P(("ka", "ia"), "ja"), P("ia", ("ka", "ja")))
     return jax.shard_map(
-        shards,
+        pick(mesh.shape["ia"], mesh.shape["ja"], mesh.shape["ka"]),
         mesh=mesh,
         in_specs=placed,
         out_specs=(P("ia", ("ka", "ja")), P("ia", ("ja", "ka")), P(("ka", "ia"), "ja")),

time: 752 us -> 296 us (0.39)
  the two profiles are of different devices: /device:TPU:27 before, /device:TPU:13 now
where the time goes in v2:
time: 296 us
  Pallas kernels  282 us (95%)
  local copies, waits for them, and re-layouts  13 us (4%)
    pallas_call x1, Pallas kernels, stationary(): pl.pallas_call(functools.partial(kernel, X, J, Z, ra, ct, rt), out_shape=...  282 us
    unnamed x3, local copies, waits for them, and re-layouts  13 us

profile of v2, /device:TPU:13, one launch (start us, length us, event | category | flops | bytes accessed | tf_op | source)
XLA Modules:
  0.0 295.7 jit_solution(9094325824548091025)
XLA Ops:
  0.6 282.0 %shard_map.58 = (bf16[512,384]{1,0:T(8,128)(2,1)}, bf16[512,1536]{1,0:T(8,128)(2,1)}, bf16[768,6144]{1,0:T(8,128)(2,1)}) custom-call(bf16[512,1536]{1,0:T(8,128)(2,1)} %pre.1, bf16[768,6144]{1,0:T(8,128)(2,1)} %w_hbm.1, bf16[512,384]{1,0:T(8,128)(2,1)} %go.1), custom_call_target="tpu_custom_call" | custom-call | tf_op jit(solution)/shard_map/pallas_call | solution.py:399
  282.6 1.8 copy.9
  284.4 2.7 copy.10
  287.1 8.6 %copy.11 = bf16[768,6144]{1,0:T(8,128)(2,1)} copy(bf16[768,6144]{1,0:T(8,128)(2,1)} %get-tuple-element.8) | data formatting | bytes 18874368

commit v3 on v2

--- a/solution.py
+++ b/solution.py
@@ -90,7 +90,7 @@
     pre_in.start()
     pl.semaphore_wait(barrier, J + has_right.astype(jnp.int32) + has_left.astype(jnp.int32))
 
-    ag_sent = []
+    ag_sent = {}
     devs = (to_right, to_left, to_px)
 
     def ag_send(p, xs, s, t, cond, own=False):
@@ -101,7 +101,7 @@
             )
 
         pl.when(cond)(lambda: copy().start())
-        ag_sent.append((cond, copy))
+        ag_sent.setdefault((xs is x, id(s)), []).append((cond, copy))
 
     def ag_got(p, xs, s):
         got(pre_all.at[xs, s, rows[p]], ag_r.at[p, xs, s])
@@ -121,44 +121,58 @@
     ag_send(1, x, z, 0, has_right, True)
     ag_send(1, x, z, 1, has_left, True)
 
-    def gb_copy(q):
-        return remote(
-            g.at[:, :, bcols], g.at[:, :, bcols], gb_s.at[q], gb_r.at[b], {"ja": lax.rem(j + q, J)}
-        )
+    mate = {"ja": j + 1 - 2 * lax.rem(j, 2)}
+    across = {"ja": lax.rem(j + 2, J)}
+    ocols = pl.ds(pl.multiple_of((nb - 1 - b) * fc, fc), fc)
+
+    def gb_copy(h, n):
+        view = g.at[h, :, bcols]
+        return remote(view, view, gb_s.at[n, h], gb_r.at[n, h], (mate, across)[n])
 
     @pl.when(home)
     def _():
         go_in.wait()
+        gb_copy(x, 1).start()
+        gb_copy(x, 0).start()
         got(g.at[px, :, bcols], go_r.at[0])
-        for q in range(1, J):
-            gb_copy(q).start()
+        gb_copy(px, 1).start()
+        gb_copy(px, 0).start()
+
+    @pl.when(jnp.logical_not(home))
+    def _():
+        for h in (x, px):
+            got(g.at[h, :, bcols], gb_r.at[1, h])
+            gb_copy(h, 0).start()
 
     ag_got(1, px, z)
     ag_send(1, px, z, 0, has_right)
     ag_send(1, px, z, 1, has_left)
 
     def ag_step(k):
-        for s, came, t, more in ((z - k, z >= k, 0, has_right), (z + k, z + k < Z, 1, has_left)):
+        sides = ((z - k, z >= k, 0, has_right), (z + k, z + k < Z, 1, has_left))
+        for s, came, t, more in sides:
             pl.when(came)(lambda s=s: ag_got(0, x, s))
+            ag_send(0, x, s, t, jnp.logical_and(came, more))
             ag_send(0, x, s, 2, came)
-            ag_send(0, x, s, t, jnp.logical_and(came, more))
             for xs in (x, px):
                 pl.when(came)(lambda s=s, xs=xs: ag_got(1, xs, s))
                 ag_send(1, xs, s, t, jnp.logical_and(came, more))
-
-    ag_step(1)
-
-    for bb in range(nb):
-        view = g.at[:, :, pl.ds(bb * fc, fc)]
-        pl.when(j != nb * x + bb)(lambda view=view, bb=bb: got(view, gb_r.at[bb]))
+        return [(s, came) for s, came, _, _ in sides]
+
+    for h in (x, px):
+        got(g.at[h, :, ocols], gb_r.at[0, h])
     w_in.wait()
 
     def r1_copy(d):
         return remote(part.at[px, d, rows[0]], r1.at[d], r1_s.at[d], r1_r.at[d], to_px)
 
-    def terms(xs, i):
-        d = jnp.where(z >= Z // 2, i, Z - 1 - i)
-
+    def far(i):
+        d = 0
+        for at in range(Z):
+            d = d + jnp.where(z == at, sorted(range(Z), key=lambda o: -abs(o - at))[i], 0)
+        return d
+
+    def terms(xs, d):
         def tile(c, carry):
             wide = pl.ds(pl.multiple_of(d * cols + c * ct, ct), ct)
             at = pl.ds(pl.multiple_of(c * ct, ct), ct)
@@ -167,18 +181,13 @@
             return carry
 
         lax.fori_loop(0, cols // ct, tile, 0)
-        return d
-
-    def terms_px(i, carry):
-        r1_copy(terms(px, i)).start()
-        return carry
-
-    def terms_x(i, carry):
-        terms(x, i)
-        return carry
-
-    lax.fori_loop(0, Z, terms_px, 0)
-    lax.fori_loop(0, Z, terms_x, 0)
+
+    terms(px, far(0))
+    r1_copy(far(0)).start()
+    for i in range(1, Z):
+        terms(px, far(i))
+    for i in range(Z):
+        terms(x, far(i))
 
     def add(dst, src, count):
         def tile(r, carry):
@@ -203,54 +212,106 @@
         got(r1.at[d], r1_r.at[d])
         add(part.at[x, d, rows[0]], r1.at[d], ra)
 
-    def rs_step(i):
-        for d, cond, more, slot, dev in (
-            (Z - 1 - i, Z - 1 - i > z, has_left, Z - 1 - i, to_right),
-            (i, i < z, has_right, jnp.where(z == i + 1, Z, i), to_left),
-        ):
+    def rs_way(right, i, cond):
+        d = Z - 1 - i if right else i
+        cond = jnp.logical_and(cond, d > z if right else d < z)
+        more = has_left if right else has_right
+        slot = d if right else jnp.where(z == i + 1, Z, i)
+        dev = to_right if right else to_left
+
+        def copy_b(xs):
+            return remote(
+                part.at[xs, d, rows[1]], rzb.at[xs, slot],
+                rb_s.at[xs, d], rb_r.at[xs, slot], dev,
+            )
+
+        def copy_a():
+            return remote(part.at[x, d, rows[0]], rza.at[slot], ra_s.at[d], ra_r.at[slot], dev)
+
+        def part_b():
             for xs in (px, x):
 
-                def copy_b(xs=xs, d=d, slot=slot, dev=dev):
-                    return remote(
-                        part.at[xs, d, rows[1]], rzb.at[xs, slot],
-                        rb_s.at[xs, d], rb_r.at[xs, slot], dev,
-                    )
-
-                pl.when(jnp.logical_and(cond, more))(lambda xs=xs, d=d: take_b(xs, d, d))
-                pl.when(cond)(lambda copy_b=copy_b: copy_b().start())
-                rs_sent.append((cond, copy_b))
-
-            def copy_a(d=d, slot=slot, dev=dev):
-                return remote(
-                    part.at[x, d, rows[0]], rza.at[slot], ra_s.at[d], ra_r.at[slot], dev
-                )
-
-            pl.when(cond)(lambda d=d: take_1(d))
-            pl.when(jnp.logical_and(cond, more))(lambda d=d: take_a(d, d))
-            pl.when(cond)(lambda copy_a=copy_a: copy_a().start())
+                @pl.when(cond)
+                def _():
+                    pl.when(more)(lambda: take_b(xs, d, d))
+                    copy_b(xs).start()
+
+                rs_sent.append((cond, lambda xs=xs: copy_b(xs)))
+
+        def part_a():
+            @pl.when(cond)
+            def _():
+                take_1(d)
+                pl.when(more)(lambda: take_a(d, d))
+                copy_a().start()
+
             rs_sent.append((cond, copy_a))
 
-    mid = Z - 2
-    for k in range(2, Z):
-        ag_step(k)
-        if k - 2 < mid:
-            rs_step(k - 2)
-
-    for s in range(Z):
-        pl.when(z != s)(lambda s=s: ag_got(0, px, s))
-    ag_got(0, px, z)
-    own_in.wait()
-    for cond, copy in ag_sent:
-        pl.when(cond)(lambda copy=copy: copy().wait_send())
-
-    def act(n, carry):
-        xs, rest = lax.div(n, Z * (tok // 16)), lax.rem(n, Z * (tok // 16))
-        s, r = lax.div(rest, tok // 16), lax.rem(rest, tok // 16)
-        at = pl.ds(pl.multiple_of(r * 16, 16), 16)
-        pre_all[xs, s, at] = gelu_value(pre_all[xs, s, at].astype(jnp.float32)).astype(jnp.bfloat16)
-        return carry
-
-    lax.fori_loop(0, X * Z * (tok // 16), act, 0)
+        return part_b, part_a
+
+    def both(way):
+        way[0]()
+        way[1]()
+
+    def act(xs, s, cond):
+        own = xs is x and s is z
+
+        def tile(r, carry):
+            at = pl.ds(pl.multiple_of(r * 16, 16), 16)
+            value = gelu_value(pre_all[xs, s, at].astype(jnp.float32))
+            pre_all[xs, s, at] = value.astype(jnp.bfloat16)
+            return carry
+
+        @pl.when(cond)
+        def _():
+            for to, copy in () if own else ag_sent[xs is x, id(s)]:
+                pl.when(to)(lambda copy=copy: copy().wait_send())
+            if xs is px:
+                ag_got(0, px, s)
+            elif own:
+                own_in.wait()
+            lax.fori_loop(0, tok // 16, tile, 0)
+
+    low, end = z < Z // 2, jnp.logical_or(z == 0, z == Z - 1)
+    inner = jnp.logical_not(end)
+    first, last = z == 0, z == Z - 1
+    ends = [(rs_way(True, i, first), rs_way(False, i, last)) for i in range(Z - 1)]
+
+    for way in ends[0]:
+        way[0]()
+    came = [ag_step(1)]
+    r1_copy(far(1)).start()
+    act(x, z, always)
+    for way in ends[0]:
+        way[1]()
+    act(px, z, always)
+    came.append(ag_step(2))
+    r1_copy(far(2)).start()
+    r1_copy(far(3)).start()
+    for way in ends[1]:
+        both(way)
+    high = jnp.logical_not(low)
+    both(rs_way(True, 0, jnp.logical_and(inner, low)))
+    both(rs_way(False, 0, jnp.logical_and(inner, high)))
+    for s, here in came[0]:
+        act(x, s, here)
+        act(px, s, here)
+    came.append(ag_step(3))
+    for way in ends[2]:
+        both(way)
+    late = (
+        rs_way(False, 0, jnp.logical_and(inner, low)),
+        rs_way(True, 0, jnp.logical_and(inner, high)),
+        rs_way(True, 1, jnp.logical_and(inner, low)),
+        rs_way(False, 1, jnp.logical_and(inner, high)),
+    )
+    for step in (0, 1):
+        for way in late:
+            way[step]()
+    for k in (1, 2):
+        for s, here in came[k]:
+            act(x, s, here)
+            act(px, s, here)
 
     def out_tile(n, carry):
         xs, r = lax.div(n, tok // rt), lax.rem(n, tok // rt)
@@ -275,9 +336,6 @@
 
     for bb in range(nb):
         pl.when(j != nb * x + bb)(lambda bb=bb: op_copy(bb).start())
-
-    for i in range(mid, Z - 1):
-        rs_step(i)
 
     for xs in range(X):
         gt[:, xs * tok : (xs + 1) * tok] = g[xs].T
@@ -369,15 +427,17 @@
     @pl.when(home)
     def _():
         ox_copy().wait_send()
-        for q in range(1, J):
-            gb_copy(q).wait_send()
+        for h in range(X):
+            gb_copy(h, 1).wait_send()
 
     for bb in range(nb):
         pl.when(j != nb * x + bb)(lambda bb=bb: op_copy(bb).wait_send())
+    for h in range(X):
+        gb_copy(h, 0).wait_send()
     rf_copy().wait_send()
     for d in range(Z):
         r1_copy(d).wait_send()
-    for cond, copy in rs_sent:
+    for cond, copy in rs_sent + ag_sent[True, id(z)]:
         pl.when(cond)(lambda copy=copy: copy().wait_send())
     for n in range(max(n_tiles - 2, 0), n_tiles):
         gw_copy(n, n % 2).wait()
@@ -419,7 +479,7 @@
             pltpu.VMEM((J - 1, X, tok, fc), half),
             pltpu.VMEM((tok, fc), half),
             pltpu.VMEM((2, feats, ct), half),
-            dma((4,)), dma((2,)), dma((1,)), dma((1,)), dma((J,)), dma((nb,)),
+            dma((4,)), dma((2,)), dma((1,)), dma((1,)), dma((2, X)), dma((2, X)),
             dma((2, X, Z, 3)), dma((2, X, Z)), dma((Z,)), dma((Z,)), dma((Z,)), dma((Z + 1,)),
             dma((X, Z)), dma((X, Z + 1)), dma((1,)), dma((1,)), dma((nb,)), dma((J,)),
             dma((1,)), dma((1,)),
@@ -432,7 +492,7 @@
 
 def pick(n_ia, n_ja, n_ka):
     def chosen(pre_act, down_weight, grad_out):
-        if n_ia == 2 and down_weight.shape[0] > pre_act.shape[0]:
+        if (n_ia, n_ja, n_ka) == (2, 4, 4) and down_weight.shape[0] > pre_act.shape[0]:
             return stationary(n_ia, n_ja, n_ka, pre_act, down_weight, grad_out)
         return shards(pre_act, down_weight, grad_out)
 

time: 296 us -> 249 us (0.84)
  the two profiles are of different devices: /device:TPU:13 before, /device:TPU:27 now
where the time goes in v3:
time: 249 us; the launch traced here: 247 us
  Pallas kernels  234 us (94%)
  local copies, waits for them, and re-layouts  13 us (5%)
    pallas_call x1, Pallas kernels, stationary(): pl.pallas_call(functools.partial(kernel, X, J, Z, ra, ct, rt), out_shape=...  234 us
    unnamed x3, local copies, waits for them, and re-layouts  13 us

profile of v3, /device:TPU:27, one launch (start us, length us, event | category | flops | bytes accessed | tf_op | source)
XLA Modules:
  0.0 247.4 jit_solution(1200729741854562793)
XLA Ops:
  0.6 233.7 %shard_map.58 = (bf16[512,384]{1,0:T(8,128)(2,1)}, bf16[512,1536]{1,0:T(8,128)(2,1)}, bf16[768,6144]{1,0:T(8,128)(2,1)}) custom-call(bf16[512,1536]{1,0:T(8,128)(2,1)} %pre.1, bf16[768,6144]{1,0:T(8,128)(2,1)} %w_hbm.1, bf16[512,384]{1,0:T(8,128)(2,1)} %go.1), custom_call_target="tpu_custom_call" | custom-call | tf_op jit(solution)/shard_map/pallas_call | solution.py:459
  234.3 1.8 copy.9
  236.1 2.7 %copy.10 = bf16[512,1536]{1,0:T(8,128)(2,1)} copy(bf16[512,1536]{1,0:T(8,128)(2,1)} %get-tuple-element.7) | data formatting | bytes 3145728
  238.8 8.6 %copy.11 = bf16[768,6144]{1,0:T(8,128)(2,1)} copy(bf16[768,6144]{1,0:T(8,128)(2,1)} %get-tuple-element.8) | data formatting | bytes 18874368

commit v4 on v3

--- a/solution.py
+++ b/solution.py
@@ -272,6 +272,34 @@
                 own_in.wait()
             lax.fori_loop(0, tok // 16, tile, 0)
 
+    n_tiles = cols // ct
+
+    def grad_cols(s, cond):
+        def copy(c):
+            wide = pl.ds(pl.multiple_of(s * cols + c * ct, ct), ct)
+            slot = lax.rem(c, 2)
+            return pltpu.make_async_copy(gwt.at[slot], gw.at[:, wide], gws.at[slot])
+
+        def tile(c, carry):
+            at = pl.ds(pl.multiple_of(c * ct, ct), ct)
+            pl.when(c >= 2)(lambda: copy(c - 2).wait())
+            acc = None
+            for xs in range(X):
+                term = jnp.dot(
+                    gt[:, xs * tok : (xs + 1) * tok], pre_all[xs, s, :, at],
+                    preferred_element_type=jnp.float32,
+                )
+                acc = term if acc is None else acc + term
+            gwt[lax.rem(c, 2)] = acc.astype(jnp.bfloat16)
+            copy(c).start()
+            return carry
+
+        @pl.when(cond)
+        def _():
+            lax.fori_loop(0, n_tiles, tile, 0)
+            for c in range(max(n_tiles - 2, 0), n_tiles):
+                copy(c).wait()
+
     low, end = z < Z // 2, jnp.logical_or(z == 0, z == Z - 1)
     inner = jnp.logical_not(end)
     first, last = z == 0, z == Z - 1
@@ -296,6 +324,15 @@
     for s, here in came[0]:
         act(x, s, here)
         act(px, s, here)
+    for xs in range(X):
+        gt[:, xs * tok : (xs + 1) * tok] = g[xs].T
+    grad_cols(z, always)
+    for s, here in came[0]:
+        grad_cols(s, here)
+    for s, here in came[1]:
+        act(x, s, jnp.logical_and(here, end))
+        act(px, s, jnp.logical_and(here, end))
+        grad_cols(s, jnp.logical_and(here, end))
     came.append(ag_step(3))
     for way in ends[2]:
         both(way)
@@ -308,13 +345,12 @@
     for step in (0, 1):
         for way in late:
             way[step]()
-    for k in (1, 2):
-        for s, here in came[k]:
-            act(x, s, here)
-            act(px, s, here)
-
-    def out_tile(n, carry):
-        xs, r = lax.div(n, tok // rt), lax.rem(n, tok // rt)
+    rest = [(s, jnp.logical_and(here, inner)) for s, here in came[1]] + came[2]
+    for s, here in rest:
+        act(x, s, here)
+        act(px, s, here)
+
+    def out_tile(xs, r):
         at = pl.ds(pl.multiple_of(r * rt, rt), rt)
         acc = None
         for s in range(Z):
@@ -325,44 +361,24 @@
             acc = term if acc is None else acc + term
         for bb in range(nb):
             outp[bb, xs, at] = acc[:, bb * fc : (bb + 1) * fc].astype(jnp.bfloat16)
+
+    def op_copy(h, n):
+        src = outp.at[(nb - 1 - b, b)[n], h]
+        return remote(src, outr.at[n, h], op_s.at[n, h], op_r.at[n, h], (mate, across)[n])
+
+    def both_halves(n, carry):
+        h = jnp.where(n == 0, px, x)
+        lax.fori_loop(0, tok // rt, lambda r, c: (out_tile(h, r), c)[1], 0)
+        op_copy(h, 0).start()
         return carry
 
-    lax.fori_loop(0, X * (tok // rt), out_tile, 0)
-
-    def op_copy(bb):
-        jd = nb * x + bb
-        q = lax.rem(j - jd - 1 + J, J)
-        return remote(outp.at[bb], outr.at[q], op_s.at[bb], op_r.at[q], {"ja": jd})
-
-    for bb in range(nb):
-        pl.when(j != nb * x + bb)(lambda bb=bb: op_copy(bb).start())
-
-    for xs in range(X):
-        gt[:, xs * tok : (xs + 1) * tok] = g[xs].T
-
-    n_tiles = Z * (cols // ct)
-
-    def gw_copy(n, slot):
-        wide = pl.ds(pl.multiple_of(n * ct, ct), ct)
-        return pltpu.make_async_copy(gwt.at[slot], gw.at[:, wide], gws.at[slot])
-
-    def gw_tile(n, carry):
-        slot = lax.rem(n, 2)
-        s, c = lax.div(n, cols // ct), lax.rem(n, cols // ct)
-        at = pl.ds(pl.multiple_of(c * ct, ct), ct)
-        pl.when(n >= 2)(lambda: gw_copy(n - 2, slot).wait())
-        acc = None
-        for xs in range(X):
-            term = jnp.dot(
-                gt[:, xs * tok : (xs + 1) * tok], pre_all[xs, s, :, at],
-                preferred_element_type=jnp.float32,
-            )
-            acc = term if acc is None else acc + term
-        gwt[slot] = acc.astype(jnp.bfloat16)
-        gw_copy(n, slot).start()
-        return carry
-
-    lax.fori_loop(0, n_tiles, gw_tile, 0)
+    lax.fori_loop(0, X, both_halves, 0)
+    for h in (px, x):
+        got(outr.at[0, h], op_r.at[0, h])
+        add(outp.at[b, h], outr.at[0, h], tok)
+        pl.when(jnp.logical_not(home))(lambda h=h: op_copy(h, 1).start())
+    for s, here in rest:
+        grad_cols(s, here)
 
     def rf_copy():
         return remote(part.at[px, z, rows[1]], rf, rf_s.at[0], rf_r.at[0], to_px)
@@ -381,29 +397,12 @@
 
     @pl.when(home)
     def _():
-        for q in range(J - 1):
-            got(outr.at[q], op_r.at[q])
-
-        def total(xs, r):
-            at = pl.ds(pl.multiple_of(r * 16, 16), 16)
-            value = outp[b, xs, at].astype(jnp.float32)
-            for q in range(J - 1):
-                value = value + outr[q, xs, at].astype(jnp.float32)
-            return at, value.astype(jnp.bfloat16)
-
-        def far(r, carry):
-            at, value = total(px, r)
-            outp[b, px, at] = value
-            return carry
-
-        def near(r, carry):
-            at, value = total(x, r)
-            out[at] = value
-            return carry
-
-        lax.fori_loop(0, tok // 16, far, 0)
+        got(outr.at[1, px], op_r.at[1, px])
+        add(outp.at[b, px], outr.at[1, px], tok)
         ox_copy().start()
-        lax.fori_loop(0, tok // 16, near, 0)
+        got(outr.at[1, x], op_r.at[1, x])
+        add(outp.at[b, x], outr.at[1, x], tok)
+        out[...] = outp[b, x]
 
     pre_in.wait()
 
@@ -423,6 +422,8 @@
         got(outx, ox_r.at[0])
         out[...] = outx[...]
         go_copy().wait_send()
+        for h in range(X):
+            op_copy(h, 1).wait_send()
 
     @pl.when(home)
     def _():
@@ -430,8 +431,8 @@
         for h in range(X):
             gb_copy(h, 1).wait_send()
 
-    for bb in range(nb):
-        pl.when(j != nb * x + bb)(lambda bb=bb: op_copy(bb).wait_send())
+    for h in range(X):
+        op_copy(h, 0).wait_send()
     for h in range(X):
         gb_copy(h, 0).wait_send()
     rf_copy().wait_send()
@@ -439,8 +440,21 @@
         r1_copy(d).wait_send()
     for cond, copy in rs_sent + ag_sent[True, id(z)]:
         pl.when(cond)(lambda copy=copy: copy().wait_send())
-    for n in range(max(n_tiles - 2, 0), n_tiles):
-        gw_copy(n, n % 2).wait()
+
+
+def hand_over(pieces, *refs):
+    sems = refs[6]
+    copies = []
+    for n in (2, 1, 0):
+        src, dst = refs[n], refs[n + 3]
+        step = src.shape[0] // pieces
+        for at in range(pieces):
+            rows = pl.ds(at * step, step)
+            copies.append(pltpu.make_async_copy(src.at[rows], dst.at[rows], sems.at[n, at]))
+    for copy in copies:
+        copy.start()
+    for copy in copies:
+        copy.wait()
 
 
 def stationary(X, J, Z, pre_act, down_weight, grad_out):
@@ -456,7 +470,7 @@
     dma = pltpu.SemaphoreType.DMA
     anywhere = pl.BlockSpec(memory_space=pl.ANY)
     vmem = pl.BlockSpec(memory_space=pltpu.VMEM)
-    return pl.pallas_call(
+    sums = pl.pallas_call(
         functools.partial(kernel, X, J, Z, ra, ct, rt),
         out_shape=(
             jax.ShapeDtypeStruct((tok, fc), half),
@@ -476,18 +490,27 @@
             pltpu.VMEM((X, Z + 1, rb, cols), half),
             pltpu.VMEM((rb, cols), half),
             pltpu.VMEM((nb, X, tok, fc), half),
-            pltpu.VMEM((J - 1, X, tok, fc), half),
+            pltpu.VMEM((2, X, tok, fc), half),
             pltpu.VMEM((tok, fc), half),
             pltpu.VMEM((2, feats, ct), half),
             dma((4,)), dma((2,)), dma((1,)), dma((1,)), dma((2, X)), dma((2, X)),
             dma((2, X, Z, 3)), dma((2, X, Z)), dma((Z,)), dma((Z,)), dma((Z,)), dma((Z + 1,)),
-            dma((X, Z)), dma((X, Z + 1)), dma((1,)), dma((1,)), dma((nb,)), dma((J,)),
+            dma((X, Z)), dma((X, Z + 1)), dma((1,)), dma((1,)), dma((2, X)), dma((2, X)),
             dma((1,)), dma((1,)),
         ],
         compiler_params=pltpu.CompilerParams(
             collective_id=0, has_side_effects=True, vmem_limit_bytes=63 * 2**20
         ),
     )(pre_act, down_weight, grad_out)
+    pieces = 8
+    return pl.pallas_call(
+        functools.partial(hand_over, pieces),
+        out_shape=tuple(jax.ShapeDtypeStruct(a.shape, a.dtype) for a in sums),
+        in_specs=[anywhere] * 3,
+        out_specs=(anywhere,) * 3,
+        scratch_shapes=[dma((3, pieces))],
+        compiler_params=pltpu.CompilerParams(vmem_limit_bytes=63 * 2**20),
+    )(*sums)
 
 
 def pick(n_ia, n_ja, n_ka):

time: 249 us -> 572 us (2.30)
  Pallas kernels: 234 us -> 571 us
  local copies, waits for them, and re-layouts: 13 us -> 0 us
    pallas_call x0 -> x1, Pallas kernels: none -> 347 us  [stationary(): pl.pallas_call(functools.partial(hand_over, pieces), out_shape=tuple((jax...]
    unnamed x3 -> x0, local copies, waits for them, and re-layouts: 13 us -> none
    pallas_call x1, Pallas kernels: 234 us -> 224 us  [stationary(): pl.pallas_call(functools.partial(kernel, X, J, Z, ra, ct, rt), out_shape=...]
where the time goes in v4:
time: 572 us
  Pallas kernels  571 us (100%)
    pallas_call x1, Pallas kernels, stationary(): pl.pallas_call(functools.partial(hand_over, pieces), out_shape=tuple((jax...  347 us
    pallas_call x1, Pallas kernels, stationary(): pl.pallas_call(functools.partial(kernel, X, J, Z, ra, ct, rt), out_shape=...  224 us

profile of v4, /device:TPU:27, one launch (start us, length us, event | category | flops | bytes accessed | tf_op | source)
XLA Modules:
  0.0 571.8 jit_solution(2017642659689576949)
XLA Ops:
  0.6 224.4 %shard_map.58 = (bf16[512,384]{1,0:T(8,128)(2,1)}, bf16[512,1536]{1,0:T(8,128)(2,1)}, bf16[768,6144]{1,0:T(8,128)(2,1)}) custom-call(bf16[512,1536]{1,0:T(8,128)(2,1)} %pre.1, bf16[768,6144]{1,0:T(8,128)(2,1)} %w_hbm.1, bf16[512,384]{1,0:T(8,128)(2,1)} %go.1), custom_call_target="tpu_custom_call" | custom-call | tf_op jit(solution)/shard_map/pallas_call | solution.py:473
  225.1 346.8 %shard_map.59 = (bf16[512,384]{1,0:T(8,128)(2,1)}, bf16[512,1536]{1,0:T(8,128)(2,1)}, bf16[768,6144]{1,0:T(8,128)(2,1)}) custom-call(bf16[512,384]{1,0:T(8,128)(2,1)} %get-tuple-element.6.refs_0_, bf16[512,1536]{1,0:T(8,128)(2,1)} %get-tuple-element.7.refs_1_, bf16[768,6144]{1,0:T(8,128)(2,1)} %get-tuple-element.8.refs_2_), custom_call_target="tpu_custom_call" | custom-call | tf_op jit(solution)/shard_map/pallas_call | solution.py:506

commit v5 on v4

--- a/solution.py
+++ b/solution.py
@@ -49,7 +49,7 @@
 def kernel(
     X, J, Z, ra, ct, rt,
     pre, w_hbm, go, out, gp, gw,
-    w, pre_all, g, gt, part, r1, rza, rzb, rf, outp, outr, outx, gwt,
+    w, pre_all, g, gt, part, r1, rza, rzb, rf, outa, outp, outr, outx, gwt,
     loc, gws, go_s, go_r, gb_s, gb_r, ag_s, ag_r, r1_s, r1_r, ra_s, ra_r, rb_s, rb_r,
     rf_s, rf_r, op_s, op_r, ox_s, ox_r,
 ):
@@ -302,6 +302,29 @@
 
     low, end = z < Z // 2, jnp.logical_or(z == 0, z == Z - 1)
     inner = jnp.logical_not(end)
+    early, last_s = jnp.where(low, 0, Z - 1), jnp.where(low, Z - 1, 0)
+
+    def out_term(xs, at, s):
+        wide = pl.ds(pl.multiple_of(s * cols, cols), cols)
+        return lax.dot_general(
+            pre_all[xs, s, at], w[:, wide], (((1,), (1,)), ((), ())),
+            preferred_element_type=jnp.float32,
+        )
+
+    def out_early(cond):
+        def tile(n, carry):
+            xs, r = lax.div(n, tok // rt), lax.rem(n, tok // rt)
+            at = pl.ds(pl.multiple_of(r * rt, rt), rt)
+            acc = out_term(xs, at, early)
+            for s in range(1, Z - 1):
+                acc = acc + out_term(xs, at, s)
+            outa[xs, at] = acc
+            return carry
+
+        @pl.when(cond)
+        def _():
+            lax.fori_loop(0, X * (tok // rt), tile, 0)
+
     first, last = z == 0, z == Z - 1
     ends = [(rs_way(True, i, first), rs_way(False, i, last)) for i in range(Z - 1)]
 
@@ -333,6 +356,7 @@
         act(x, s, jnp.logical_and(here, end))
         act(px, s, jnp.logical_and(here, end))
         grad_cols(s, jnp.logical_and(here, end))
+    out_early(end)
     came.append(ag_step(3))
     for way in ends[2]:
         both(way)
@@ -345,6 +369,7 @@
     for step in (0, 1):
         for way in late:
             way[step]()
+    out_early(inner)
     rest = [(s, jnp.logical_and(here, inner)) for s, here in came[1]] + came[2]
     for s, here in rest:
         act(x, s, here)
@@ -352,13 +377,7 @@
 
     def out_tile(xs, r):
         at = pl.ds(pl.multiple_of(r * rt, rt), rt)
-        acc = None
-        for s in range(Z):
-            term = lax.dot_general(
-                pre_all[xs, s, at], w[:, s * cols : (s + 1) * cols], (((1,), (1,)), ((), ())),
-                preferred_element_type=jnp.float32,
-            )
-            acc = term if acc is None else acc + term
+        acc = outa[xs, at] + out_term(xs, at, last_s)
         for bb in range(nb):
             outp[bb, xs, at] = acc[:, bb * fc : (bb + 1) * fc].astype(jnp.bfloat16)
 
@@ -392,6 +411,15 @@
     pl.when(has_left)(lambda: take_a(z, z))
     pl.when(has_right)(lambda: take_a(z, Z))
 
+    pre_in.wait()
+
+    def slope(r, carry):
+        at = pl.ds(pl.multiple_of(r * 16, 16), 16)
+        value = part[x, z, at].astype(jnp.float32) * gelu_slope(gp[at].astype(jnp.float32))
+        gp[at] = value.astype(jnp.bfloat16)
+        return carry
+
+    lax.fori_loop(0, ra // 16, slope, 0)
     def ox_copy():
         return remote(outp.at[b, px], outx, ox_s.at[0], ox_r.at[0], to_px)
 
@@ -404,15 +432,6 @@
         add(outp.at[b, x], outr.at[1, x], tok)
         out[...] = outp[b, x]
 
-    pre_in.wait()
-
-    def slope(r, carry):
-        at = pl.ds(pl.multiple_of(r * 16, 16), 16)
-        value = part[x, z, at].astype(jnp.float32) * gelu_slope(gp[at].astype(jnp.float32))
-        gp[at] = value.astype(jnp.bfloat16)
-        return carry
-
-    lax.fori_loop(0, ra // 16, slope, 0)
     got(rf, rf_r.at[0])
     add(part.at[x, z, rows[1]], rf, tok - ra)
     lax.fori_loop(ra // 16, tok // 16, slope, 0)
@@ -443,18 +462,23 @@
 
 
 def hand_over(pieces, *refs):
-    sems = refs[6]
+    held, sems = refs[6:9], refs[9]
     copies = []
     for n in (2, 1, 0):
-        src, dst = refs[n], refs[n + 3]
+        src, dst, mid = refs[n], refs[n + 3], held[n]
         step = src.shape[0] // pieces
         for at in range(pieces):
             rows = pl.ds(at * step, step)
-            copies.append(pltpu.make_async_copy(src.at[rows], dst.at[rows], sems.at[n, at]))
-    for copy in copies:
-        copy.start()
-    for copy in copies:
-        copy.wait()
+            come = pltpu.make_async_copy(src.at[rows], mid.at[rows], sems.at[0, n, at])
+            leave = pltpu.make_async_copy(mid.at[rows], dst.at[rows], sems.at[1, n, at])
+            copies.append((come, leave))
+    for come, _ in copies:
+        come.start()
+    for come, leave in copies:
+        come.wait()
+        leave.start()
+    for _, leave in copies:
+        leave.wait()
 
 
 def stationary(X, J, Z, pre_act, down_weight, grad_out):
@@ -489,6 +513,7 @@
             pltpu.VMEM((Z + 1, ra, cols), half),
             pltpu.VMEM((X, Z + 1, rb, cols), half),
             pltpu.VMEM((rb, cols), half),
+            pltpu.VMEM((X, tok, nb * fc), jnp.float32),
             pltpu.VMEM((nb, X, tok, fc), half),
             pltpu.VMEM((2, X, tok, fc), half),
             pltpu.VMEM((tok, fc), half),
@@ -508,7 +533,7 @@
         out_shape=tuple(jax.ShapeDtypeStruct(a.shape, a.dtype) for a in sums),
         in_specs=[anywhere] * 3,
         out_specs=(anywhere,) * 3,
-        scratch_shapes=[dma((3, pieces))],
+        scratch_shapes=[pltpu.VMEM(a.shape, a.dtype) for a in sums] + [dma((2, 3, pieces))],
         compiler_params=pltpu.CompilerParams(vmem_limit_bytes=63 * 2**20),
     )(*sums)
 

time: 572 us -> 227 us (0.40)
  Pallas kernels: 571 us -> 226 us
    pallas_call x1, Pallas kernels: 347 us -> 8.38 us  [stationary(): pl.pallas_call(functools.partial(hand_over, pieces), out_shape=tuple((jax...]
    pallas_call x1, Pallas kernels: 224 us -> 217 us  [stationary(): pl.pallas_call(functools.partial(kernel, X, J, Z, ra, ct, rt), out_shape=...]
where the time goes in v5:
time: 227 us
  Pallas kernels  226 us (100%)
    pallas_call x1, Pallas kernels, stationary(): pl.pallas_call(functools.partial(kernel, X, J, Z, ra, ct, rt), out_shape=...  217 us
    pallas_call x1, Pallas kernels, stationary(): pl.pallas_call(functools.partial(hand_over, pieces), out_shape=tuple((jax...  8.38 us

profile of v5, /device:TPU:27, one launch (start us, length us, event | category | flops | bytes accessed | tf_op | source)
XLA Modules:
  0.0 226.5 jit_solution(144942108343354662)
XLA Ops:
  0.6 217.3 %shard_map.58 = (bf16[512,384]{1,0:T(8,128)(2,1)}, bf16[512,1536]{1,0:T(8,128)(2,1)}, bf16[768,6144]{1,0:T(8,128)(2,1)}) custom-call(bf16[512,1536]{1,0:T(8,128)(2,1)} %pre.1, bf16[768,6144]{1,0:T(8,128)(2,1)} %w_hbm.1, bf16[512,384]{1,0:T(8,128)(2,1)} %go.1), custom_call_target="tpu_custom_call" | custom-call | tf_op jit(solution)/shard_map/pallas_call | solution.py:497
  218.0 8.4 %shard_map.59 = (bf16[512,384]{1,0:T(8,128)(2,1)}, bf16[512,1536]{1,0:T(8,128)(2,1)}, bf16[768,6144]{1,0:T(8,128)(2,1)}) custom-call(bf16[512,384]{1,0:T(8,128)(2,1)} %get-tuple-element.6.refs_0_, bf16[512,1536]{1,0:T(8,128)(2,1)} %get-tuple-element.7.refs_1_, bf16[768,6144]{1,0:T(8,128)(2,1)} %get-tuple-element.8.refs_2_), custom_call_target="tpu_custom_call" | custom-call | tf_op jit(solution)/shard_map/pallas_call | solution.py:531
